TPU v7x, 32 devices: a whole 2x2x4 slice. The times are simulated.
32 devices in a mesh: groups: 2 (over x), ty: 16 (over z, y, core).
Axes of the slice: x: 2, y: 2, z: 4, core: 2. Of those that a mesh axis runs over, the one named last changes fastest.
Arguments:
- transmission: bfloat16 [4, 2, 8192, 1024], P(None, None, ('groups', 'ty')), parts along dimension 2, may hold values from -4 to 4
- probe_wavefield: float32 [4, 128, 128], P('groups'), parts along dimension 0, may hold values from -6 to 6
- phase_shift: float32 [128, 128], replicated, may hold values from -3.140625 to 3.140625
- offsets: int32 [2, 256], P(None, ('groups', 'ty')), parts along dimension 1, may hold values from 0 to 3968, as said below
- live_counts: int32 [32], P('groups'), parts along dimension 0, may hold values from 0 to 8, as said below
- measured: bfloat16 [256, 128, 128], P(('groups', 'ty')), parts along dimension 0, may hold values from 1 to 9, as said below
Outputs:
- object_grad: float32 [4, 2, 8192, 1024], P(None, None, ('groups', 'ty')), parts along dimension 2
- probe_grad: float32 [4, 128, 128], P('groups'), parts along dimension 0
There are 2 independent parts, one for each index of `groups`. A program takes and returns all parts, laid end to end along the dimension named above; an argument that names none is the same for every part. Nothing has to cross between parts.
Inputs may be any that keep to these rules, and one draw needn't show every extreme that they name: Slot p belongs to device p // 8 along ty; its row offset lies within that device's 256 tile rows and its window stays inside the object; column offsets run from 0 to 896. `live_counts`: the live slots of a device are its first ones; on each aligned pair of devices 2k and 2k+1 along ty the two counts add up to 8. `measured`: positive amplitudes.
All inputs are finite; a program needn't handle non-finite values.
Results may differ from a plain program's by a relative error of at most 0.03.
The roundings to bfloat16 on the way count: a program that leaves them out, or rounds other values in their place, can miss the bound.
Values may be sent and summed in bfloat16 or wider, within the bound.
No kernel may reach another device: no remote copies, remote signals or barrier semaphores. Data moves between devices by JAX's collectives and lax.ppermute only.
A program may use at most 128 MiB of HBM per device.

v0:
```python
import math

import jax
import jax.numpy as jnp
from jax import lax
from jax.sharding import PartitionSpec as P

RIDGE = 0.25


def passed_along(block, axis, distance):
    devices = range(lax.axis_size(axis))
    route = [(i - distance, i) for i in devices if i - distance in devices]
    return lax.ppermute(block, axis, route)


def dft_tables(patch_size, sign):
    positions = jnp.arange(patch_size, dtype=jnp.int32)
    product = positions[:, None] * positions[None, :] % patch_size
    angles = 2.0 * math.pi / patch_size * product.astype(jnp.float32)
    normalizer = 1.0 / math.sqrt(patch_size)
    table_real = jnp.cos(angles) * normalizer
    table_imag = sign * jnp.sin(angles) * normalizer
    left_table = jnp.concatenate(
        [
            jnp.concatenate([table_real, -table_imag], 1),
            jnp.concatenate([table_imag, table_real], 1),
        ],
        0,
    )
    right_table = jnp.concatenate(
        [
            jnp.concatenate([table_real, table_imag], 1),
            jnp.concatenate([-table_imag, table_real], 1),
        ],
        0,
    )
    return (left_table.astype(jnp.bfloat16), right_table.astype(jnp.bfloat16))


def transform(wave_real, wave_imag, tables):
    left_table, right_table = tables
    patch_size = wave_real.shape[0]
    stacked = jnp.concatenate([wave_real, wave_imag], 0).astype(jnp.bfloat16)
    halfway = jnp.dot(left_table, stacked, preferred_element_type=jnp.float32).astype(jnp.bfloat16)
    side_by_side = jnp.concatenate([halfway[:patch_size], halfway[patch_size:]], 1)
    result = jnp.dot(side_by_side, right_table, preferred_element_type=jnp.float32)
    return (result[:, :patch_size], result[:, patch_size:])


def position_loss(
    object_window,
    probe_wavefield,
    measured,
    kernel_real_part,
    kernel_imaginary,
    forward_transform,
    inverse_transform,
):
    wave_real, wave_imag = (probe_wavefield[0], probe_wavefield[1])
    slices = object_window.shape[0]
    for slice_id in range(slices):
        layer_real, layer_imag = (object_window[slice_id, 0], object_window[slice_id, 1])
        wave_real, wave_imag = (
            wave_real * layer_real - wave_imag * layer_imag,
            wave_real * layer_imag + wave_imag * layer_real,
        )
        if slice_id + 1 < slices:
            freq_real, freq_imag = transform(wave_real, wave_imag, forward_transform)
            freq_real, freq_imag = (
                freq_real * kernel_real_part - freq_imag * kernel_imaginary,
                freq_real * kernel_imaginary + freq_imag * kernel_real_part,
            )
            wave_real, wave_imag = transform(freq_real, freq_imag, inverse_transform)
    far_real, far_imag = transform(wave_real, wave_imag, forward_transform)
    amplitude = jnp.sqrt(far_real * far_real + far_imag * far_imag + RIDGE)
    return jnp.sum((amplitude - measured.astype(jnp.float32)) ** 2)


def cut_windows(extended, row_start, col_start, patch_size):
    zero_index = jnp.zeros((), jnp.int32)

    def cut_single(single_row, single_column):
        return lax.dynamic_slice(
            extended,
            (zero_index, zero_index, single_row, single_column),
            (extended.shape[0], 2, patch_size, patch_size),
        )

    return jax.vmap(cut_single)(row_start, col_start)


def window_grads(
    windows, probe_wavefield, measured, weights, kernels, forward_transform, inverse_transform
):
    gradient_function = jax.grad(position_loss, argnums=(0, 1))

    def window_single(object_window, single_measurement, single_weight):
        window_gradient, probe_gradient = gradient_function(
            object_window.astype(jnp.float32),
            probe_wavefield,
            single_measurement,
            kernels[0],
            kernels[1],
            forward_transform,
            inverse_transform,
        )
        return (window_gradient * single_weight, probe_gradient * single_weight)

    g_windows, g_probes = jax.vmap(window_single)(windows, measured, weights)
    return (g_windows, jnp.sum(g_probes, 0))


def local(transmission, probe_wavefield, phase_shift, offsets, live_counts, measured):
    slices = transmission.shape[0]
    tile_rows = transmission.shape[2]
    tile_width = transmission.shape[3]
    patch_size = probe_wavefield.shape[-1]
    capacity = offsets.shape[1]
    devices = lax.axis_size("ty")
    my_index = lax.axis_index("ty")
    forward_transform = dft_tables(patch_size, -1.0)
    inverse_transform = dft_tables(patch_size, 1.0)
    kernels = (jnp.cos(phase_shift), jnp.sin(phase_shift))
    below = passed_along(transmission[:, :, :patch_size, :], "ty", -1)
    extended = jnp.concatenate([transmission, below], 2)
    row_start = offsets[0] - my_index * tile_rows
    col_start = offsets[1]
    windows = cut_windows(extended, row_start, col_start, patch_size)
    own_live = live_counts[my_index]
    slot_ids = jnp.arange(capacity, dtype=jnp.int32)
    weights = (slot_ids < own_live).astype(jnp.float32)
    slot_grads, probe_part = window_grads(
        windows, probe_wavefield, measured, weights, kernels, forward_transform, inverse_transform
    )
    zero_index = jnp.zeros((), jnp.int32)

    def deposit(slot_id, grad_acc):
        corner = (zero_index, zero_index, row_start[slot_id], col_start[slot_id])
        current = lax.dynamic_slice(grad_acc, corner, slot_grads.shape[1:])
        return lax.dynamic_update_slice(grad_acc, current + slot_grads[slot_id], corner)

    grad_acc = lax.fori_loop(
        0,
        capacity,
        deposit,
        jnp.zeros((slices, 2, tile_rows + patch_size, tile_width), jnp.float32),
    )
    incoming_rim = passed_along(grad_acc[:, :, tile_rows:, :].astype(jnp.bfloat16), "ty", 1).astype(
        jnp.float32
    )
    object_grad = grad_acc[:, :, :tile_rows, :].at[:, :, :patch_size, :].add(incoming_rim)
    probe_grad = lax.psum(probe_part, "ty") / math.sqrt(capacity * devices)
    return (object_grad, probe_grad)


def solution(mesh):
    in_specs = (
        P(None, None, ("groups", "ty"), None),
        P("groups", None, None),
        P(),
        P(None, ("groups", "ty")),
        P("groups"),
        P(("groups", "ty"), None, None),
    )
    out_specs = (P(None, None, ("groups", "ty"), None), P("groups", None, None))
    return jax.shard_map(local, mesh=mesh, in_specs=in_specs, out_specs=out_specs, check_vma=False)
```

profile of v0, /device:TPU:8, one launch (start us, length us, event | category | flops | bytes accessed | tf_op | source)
XLA Modules:
  0.0 342.9 jit_solution(12836923129339388549)
XLA Ops:
  9.2 2.8 collective-permute-start
  14.6 20.8 %collective-permute-done = bf16[4,2,128,1024]{3,2,1,0:T(8,128)(2,1)} collective-permute-done((bf16[4,2,128,1024]{3,2,1,0:T(8,128)(2,1)S(1)}, bf16[4,2,128,1024]{3,2,1,0:T(8,128)(2,1)}, u32[]{:S(2)}, u32[]{:S(2)}) %collective-permute-start) | collective-permute-done | bytes 2097184 | tf_op jit(solution)/shard_map/ppermute | solution.py:14
  35.5 6.2 %pad_maximum_fusion = bf16[4,2,384,1024]{3,2,1,0:T(8,128)(2,1)} fusion(bf16[4,2,128,1024]{3,2,1,0:T(8,128)(2,1)} %collective-permute-done, bf16[4,2,256,1024]{3,2,1,0:T(8,128)(2,1)} %param.10), kind=kLoop, calls=%fused_computation.5 | loop fusion | flops 12582912 | bytes 12582912 | tf_op jit(solution)/shard_map/concatenate | solution.py:126
  41.7 33.6 %while.16 = (s32[]{:T(128)}, bf16[4,2,384,1024]{3,2,1,0:T(8,128)(2,1)}, s32[8,4]{0,1:T(4,128)S(1)}, bf16[8,4,2,128,128]{3,4,0,2,1:T(8,128)(2,1)}, s32[]{:T(128)}) while((s32[]{:T(128)}, bf16[4,2,384,1024]{3,2,1,0:T(8,128)(2,1)}, s32[8,4]{0,1:T(4,128)S(1)}, bf16[8,4,2,128,128]{3,4,0,2,1:T(8,128)(2,1)}, s32[]{:T(128)}) %tuple.100), condition=%wide.while_cond.1, body=%wide.while_body.1.sunk | while | flops 2 | bytes 1572997 | solution.py:84
  42.4 2.6 dynamic-slice_bitcast_fusion.2
  59.1 2.6 dynamic-slice_bitcast_fusion.2
  63.3 2.6 dynamic-slice_bitcast_fusion.2
  67.5 2.6 dynamic-slice_bitcast_fusion.2
  71.7 2.6 dynamic-slice_bitcast_fusion.2
  100.7 6.2 %broadcast_in_dim.22 = f32[4,2,384,1024]{3,2,1,0:T(8,128)} broadcast(f32[]{:T(128)} %constant.98.clone.1), dimensions={} | broadcast | bytes 12582916 | tf_op jit(solution)/shard_map/broadcast_in_dim | solution.py:147
  106.8 122.6 %while.15 = (s32[]{:T(128)}, f32[4,2,384,1024]{3,2,1,0:T(8,128)}, s32[8]{0:T(128)S(1)}, s32[8]{0:T(128)S(1)}, f32[8,4,2,128,128]{3,4,0,2,1:T(8,128)}, /*index=5*/s32[]{:T(128)}, s32[]{:T(128)}, s32[]{:T(128)}, s32[]{:T(128)}) while((s32[]{:T(128)}, f32[4,2,384,1024]{3,2,1,0:T(8,128)}, s32[8]{0:T(128)S(1)}, s32[8]{0:T(128)S(1)}, ...), condition=%wide.region_1.2_spmd, body=%wide.region_0.1_spmd.sunk | while | flops 131080 | bytes 4718801 | solution.py:143
  114.7 7.7 %dynamic_update_slice.8 = f32[4,2,384,1024]{3,2,1,0:T(8,128)} dynamic-update-slice(f32[4,2,384,1024]{3,2,1,0:T(8,128)} %get-tuple-element.320, f32[4,2,128,128]{3,2,1,0:T(8,128)S(1)} %bitcast_add_fusion.2, s32[]{:T(128)} %constant.97.clone.1..sunk, s32[]{:T(128)} %constant.97.clone.1..sunk, s32[]{:T(128)S(6)} %select_n.110, s32[]{:T(128)S(6)} %select_n.111) | dynamic-update-slice | bytes 1048580 | tf_op jit(solution)/shard_map/while/body/eval_jaxpr/dynamic_update_slice | solution.py:141
  130.3 7.6 %dynamic_update_slice.8 = f32[4,2,384,1024]{3,2,1,0:T(8,128)} dynamic-update-slice(f32[4,2,384,1024]{3,2,1,0:T(8,128)} %get-tuple-element.320, f32[4,2,128,128]{3,2,1,0:T(8,128)S(1)} %bitcast_add_fusion.2, s32[]{:T(128)} %constant.97.clone.1..sunk, s32[]{:T(128)} %constant.97.clone.1..sunk, s32[]{:T(128)S(6)} %select_n.110, s32[]{:T(128)S(6)} %select_n.111) | dynamic-update-slice | bytes 1048580 | tf_op jit(solution)/shard_map/while/body/eval_jaxpr/dynamic_update_slice | solution.py:141
  145.7 7.7 %dynamic_update_slice.8 = f32[4,2,384,1024]{3,2,1,0:T(8,128)} dynamic-update-slice(f32[4,2,384,1024]{3,2,1,0:T(8,128)} %get-tuple-element.320, f32[4,2,128,128]{3,2,1,0:T(8,128)S(1)} %bitcast_add_fusion.2, s32[]{:T(128)} %constant.97.clone.1..sunk, s32[]{:T(128)} %constant.97.clone.1..sunk, s32[]{:T(128)S(6)} %select_n.110, s32[]{:T(128)S(6)} %select_n.111) | dynamic-update-slice | bytes 1048580 | tf_op jit(solution)/shard_map/while/body/eval_jaxpr/dynamic_update_slice | solution.py:141
  161.3 7.7 %dynamic_update_slice.8 = f32[4,2,384,1024]{3,2,1,0:T(8,128)} dynamic-update-slice(f32[4,2,384,1024]{3,2,1,0:T(8,128)} %get-tuple-element.320, f32[4,2,128,128]{3,2,1,0:T(8,128)S(1)} %bitcast_add_fusion.2, s32[]{:T(128)} %constant.97.clone.1..sunk, s32[]{:T(128)} %constant.97.clone.1..sunk, s32[]{:T(128)S(6)} %select_n.110, s32[]{:T(128)S(6)} %select_n.111) | dynamic-update-slice | bytes 1048580 | tf_op jit(solution)/shard_map/while/body/eval_jaxpr/dynamic_update_slice | solution.py:141
  176.9 7.7 %dynamic_update_slice.8 = f32[4,2,384,1024]{3,2,1,0:T(8,128)} dynamic-update-slice(f32[4,2,384,1024]{3,2,1,0:T(8,128)} %get-tuple-element.320, f32[4,2,128,128]{3,2,1,0:T(8,128)S(1)} %bitcast_add_fusion.2, s32[]{:T(128)} %constant.97.clone.1..sunk, s32[]{:T(128)} %constant.97.clone.1..sunk, s32[]{:T(128)S(6)} %select_n.110, s32[]{:T(128)S(6)} %select_n.111) | dynamic-update-slice | bytes 1048580 | tf_op jit(solution)/shard_map/while/body/eval_jaxpr/dynamic_update_slice | solution.py:141
  192.5 7.0 %dynamic_update_slice.8 = f32[4,2,384,1024]{3,2,1,0:T(8,128)} dynamic-update-slice(f32[4,2,384,1024]{3,2,1,0:T(8,128)} %get-tuple-element.320, f32[4,2,128,128]{3,2,1,0:T(8,128)S(1)} %bitcast_add_fusion.2, s32[]{:T(128)} %constant.97.clone.1..sunk, s32[]{:T(128)} %constant.97.clone.1..sunk, s32[]{:T(128)S(6)} %select_n.110, s32[]{:T(128)S(6)} %select_n.111) | dynamic-update-slice | bytes 1048580 | tf_op jit(solution)/shard_map/while/body/eval_jaxpr/dynamic_update_slice | solution.py:141
  207.3 6.9 %dynamic_update_slice.8 = f32[4,2,384,1024]{3,2,1,0:T(8,128)} dynamic-update-slice(f32[4,2,384,1024]{3,2,1,0:T(8,128)} %get-tuple-element.320, f32[4,2,128,128]{3,2,1,0:T(8,128)S(1)} %bitcast_add_fusion.2, s32[]{:T(128)} %constant.97.clone.1..sunk, s32[]{:T(128)} %constant.97.clone.1..sunk, s32[]{:T(128)S(6)} %select_n.110, s32[]{:T(128)S(6)} %select_n.111) | dynamic-update-slice | bytes 1048580 | tf_op jit(solution)/shard_map/while/body/eval_jaxpr/dynamic_update_slice | solution.py:141
  222.1 7.3 %dynamic_update_slice.8 = f32[4,2,384,1024]{3,2,1,0:T(8,128)} dynamic-update-slice(f32[4,2,384,1024]{3,2,1,0:T(8,128)} %get-tuple-element.320, f32[4,2,128,128]{3,2,1,0:T(8,128)S(1)} %bitcast_add_fusion.2, s32[]{:T(128)} %constant.97.clone.1..sunk, s32[]{:T(128)} %constant.97.clone.1..sunk, s32[]{:T(128)S(6)} %select_n.110, s32[]{:T(128)S(6)} %select_n.111) | dynamic-update-slice | bytes 1048580 | tf_op jit(solution)/shard_map/while/body/eval_jaxpr/dynamic_update_slice | solution.py:141
  229.5 3.8 %slice.397 = bf16[4,2,128,1024]{3,2,1,0:T(8,128)(2,1)} slice(f32[4,2,384,1024]{3,2,1,0:T(8,128)} %get-tuple-element.108), slice={[0:4], [0:2], [256:384], [0:1024]} | slice | bytes 4194304 | tf_op jit(solution)/shard_map/slice | solution.py:149
  233.3 4.6 %collective-permute-start.1 = (bf16[4,2,128,1024]{3,2,1,0:T(8,128)(2,1)}, bf16[4,2,128,1024]{3,2,1,0:T(8,128)(2,1)S(1)}, u32[]{:S(2)}, u32[]{:S(2)}) collective-permute-start(bf16[4,2,128,1024]{3,2,1,0:T(8,128)(2,1)} %slice.397), channel_id=1, source_target_pairs={{0,1},{1,2},{2,3},{3,4},{4,5},{5,6},{6,7},{7,8},{8,9},{9,10},{10,1... | collective-permute-start | bytes 6291464 | tf_op jit(solution)/shard_map/ppermute | solution.py:14
  238.7 8.4 %slice.201 = f32[4,2,256,1024]{3,2,1,0:T(8,128)} slice(f32[4,2,384,1024]{3,2,1,0:T(8,128)} %get-tuple-element.108), slice={[0:4], [0:2], [0:256], [0:1024]} | slice | bytes 16777216 | tf_op jit(solution)/shard_map/slice | solution.py:152
  247.1 82.0 %all-reduce.40.cloned.1.call-done = f32[2,128,128]{1,2,0:T(8,128)} async-done(((f32[2,128,128]{1,2,0:T(8,128)}), f32[2,128,128]{1,2,0:T(8,128)}) %all-reduce.40.cloned.1.call-update) | async-done | bytes 131088 | tf_op jit(solution)/shard_map/psum | solution.py:153
  330.8 5.3 %add_dynamic-update-slice_fusion = f32[4,2,256,1024]{3,2,1,0:T(8,128)} fusion(f32[4,2,256,1024]{3,2,1,0:T(8,128)} %slice.201, bf16[4,2,128,1024]{3,2,1,0:T(8,128)(2,1)S(1)} %collective-permute-done.1, f32[4,2,384,1024]{3,2,1,0:T(8,128)} %get-tuple-element.108), kind=kLoop, calls=%fused_computation.7 | loop fusion | flops 2097152 | bytes 10485760 | tf_op jit(solution)/shard_map/scatter-add | solution.py:152
  (191 shorter events, 84.1 us)
Async XLA Ops:
  7.2 4.8 %copy-start.5 = (f32[2,128,128]{2,1,0:T(8,128)S(1)}, f32[2,128,128]{2,1,0:T(8,128)}, u32[]{:S(2)}) copy-start(f32[2,128,128]{2,1,0:T(8,128)} %param.11) | copy-start | bytes 393220
  7.2 5.0 %copy-start.8 = (s32[16]{0:T(128)S(1)}, s32[16]{0:T(128)}, u32[]{:S(2)}) copy-start(s32[16]{0:T(128)} %param.14) | copy-start | bytes 196
  7.2 7.1 %copy-start.7 = (s32[2,8]{1,0:T(2,128)S(1)}, s32[2,8]{1,0:T(2,128)}, u32[]{:S(2)}) copy-start(s32[2,8]{1,0:T(2,128)} %param.13) | copy-start | bytes 196
  7.2 7.2 %copy-start.6 = (f32[128,128]{1,0:T(8,128)S(1)}, f32[128,128]{1,0:T(8,128)}, u32[]{:S(2)}) copy-start(f32[128,128]{1,0:T(8,128)} %param.12) | copy-start | bytes 196612
  7.2 322.0 %all-reduce.40.cloned.1.call-start = ((), (), s32[]{:S(2)}) async-start(), calls=%async_computation | async-start | bytes 262144 | tf_op jit(solution)/shard_map/psum | solution.py:153
  9.2 26.3 %collective-permute-start = (bf16[4,2,128,1024]{3,2,1,0:T(8,128)(2,1)S(1)}, bf16[4,2,128,1024]{3,2,1,0:T(8,128)(2,1)}, u32[]{:S(2)}, u32[]{:S(2)}) collective-permute-start(bf16[4,2,128,1024]{3,2,1,0:T(8,128)(2,1)S(1)} %slice.163), channel_id=1, source_target_pairs={{1,0},{2,1},{3,2},{4,3},{5,4},{6,5},{7,6},{8,7},{9,8},{10,9},{11,1... | collective-permute-start | bytes 6291464 | tf_op jit(solution)/shard_map/ppermute | solution.py:14
  12.2 65.2 %copy-start.2 = (f32[128,128]{0,1:T(8,128)}, f32[128,128]{0,1:T(8,128)S(1)}, u32[]{:S(2)}) copy-start(f32[128,128]{0,1:T(8,128)S(1)} %copy.43) | copy-start | bytes 196612
  77.4 2.0 copy-start
  87.0 2.2 copy-start.1
  89.2 1.1 copy-start.4
  96.5 1.6 copy-start.3
  233.3 97.6 %collective-permute-start.1 = (bf16[4,2,128,1024]{3,2,1,0:T(8,128)(2,1)}, bf16[4,2,128,1024]{3,2,1,0:T(8,128)(2,1)S(1)}, u32[]{:S(2)}, u32[]{:S(2)}) collective-permute-start(bf16[4,2,128,1024]{3,2,1,0:T(8,128)(2,1)} %slice.397), channel_id=1, source_target_pairs={{0,1},{1,2},{2,3},{3,4},{4,5},{5,6},{6,7},{7,8},{8,9},{9,10},{10,1... | collective-permute-start | bytes 6291464 | tf_op jit(solution)/shard_map/ppermute | solution.py:14
Sparse Core Ops, SparseCore 0:
  238.8 90.3 all-reduce.39
where the time goes:
time: 347 us; the launch traced here: 343 us
  local copies, waits for them, and re-layouts  140 us (40%)
  waiting for transfers between devices  103 us (30%)
  other arithmetic  37.2 us (11%)
  loops' own time  31.3 us (9%)
  between operations  14.7 us (4%)
  matrix products  9.75 us (3%)
  starting transfers between devices  7.37 us (2%)
    psum x1, waiting for transfers between devices, local(): probe_grad = lax.psum(probe_part, 'ty') / math.sqrt(capacity * devices)  82 us
    dynamic_update_slice x8, local copies, waits for them, and re-layouts, deposit(): lax.dynamic_update_slice(grad_acc, current + slot_grads[slot_id], corner)  59.9 us
    gather x40, local copies, waits for them, and re-layouts  33.5 us
    another operation x1, loops' own time, local(): lax.fori_loop(0, capacity, deposit, jnp.zeros((slices, 2, tile_rows + pat...  31.2 us
    ppermute x2, waiting for transfers between devices, passed_along(): return lax.ppermute(block, axis, route)  20.8 us
    add x8, other arithmetic, deposit(): current + slot_grads[slot_id]  11.9 us
    dynamic_slice x16, local copies, waits for them, and re-layouts, deposit(): slot_grads[slot_id]  10.3 us
    dynamic_slice x16, local copies, waits for them, and re-layouts, deposit(): corner = (zero_index, zero_index, row_start[slot_id], col_start[slot_id])  9.37 us
  transfers between devices with their start and end apart: 3, of which 2 were waited for; matrix products, arithmetic and copies ran while one was open for 4% of the time, Pallas kernels for 0%

commit v1 on v0

v1 whole, which is shorter than its diff:
```python
import math

import jax
import jax.numpy as jnp
import numpy as np
from jax import lax
from jax.experimental import pallas as pl
from jax.experimental.pallas import tpu as pltpu
from jax.sharding import PartitionSpec as P

RIDGE = 0.25
GROUP = 4
LANES = 128


def passed_along(block, axis, distance):
    devices = range(lax.axis_size(axis))
    route = [(i - distance, i) for i in devices if i - distance in devices]
    return lax.ppermute(block, axis, route)


def summed_over(block, axis):
    devices = lax.axis_size(axis)
    if devices & (devices - 1):
        return lax.psum(block, axis)
    step = 1
    while step < devices:
        route = [(i, i ^ step) for i in range(devices)]
        block = block.astype(jnp.bfloat16)
        other = lax.ppermute(block, axis, route)
        block = block.astype(jnp.float32) + other.astype(jnp.float32)
        step *= 2
    return block


def dft_tables(patch_size):
    positions = np.arange(patch_size)
    product = positions[:, None] * positions[None, :] % patch_size
    angles = 2.0 * math.pi / patch_size * product
    real = np.cos(angles) / math.sqrt(patch_size)
    imag = -np.sin(angles) / math.sqrt(patch_size)
    left = np.block([[real, -imag], [imag, real]])
    return (jnp.asarray(left, jnp.bfloat16), jnp.asarray(left.T, jnp.bfloat16))


def matmul(a, b):
    return jnp.dot(a, b, preferred_element_type=jnp.float32)


def swap_halves(block, n):
    return jnp.concatenate(
        [
            jnp.concatenate([block[:n, :n], block[n:, :n]], 1),
            jnp.concatenate([block[:n, n:], block[n:, n:]], 1),
        ],
        0,
    )


def transform_pairs(fields, left, right):
    out = []
    for k in range(0, len(fields), 2):
        (a_re, a_im), (b_re, b_im) = fields[k], fields[k + 1]
        n = a_re.shape[0]
        stacked = jnp.concatenate(
            [
                jnp.concatenate([a_re, a_im], 0).astype(jnp.bfloat16),
                jnp.concatenate([b_re, b_im], 0).astype(jnp.bfloat16),
            ],
            1,
        )
        halfway = matmul(left, stacked).astype(jnp.bfloat16)
        result = matmul(swap_halves(halfway, n), right)
        out += [(result[:n, :n], result[:n, n:]), (result[n:, :n], result[n:, n:])]
    return out


def transform_pairs_back(grads, left, right):
    out = []
    for k in range(0, len(grads), 2):
        (a_re, a_im), (b_re, b_im) = grads[k], grads[k + 1]
        n = a_re.shape[0]
        side = jnp.concatenate(
            [
                jnp.concatenate([a_re, a_im], 1).astype(jnp.bfloat16),
                jnp.concatenate([b_re, b_im], 1).astype(jnp.bfloat16),
            ],
            0,
        )
        halfway = matmul(side, right).astype(jnp.bfloat16)
        stacked = jnp.concatenate(
            [
                jnp.concatenate([halfway[:n, :n], halfway[:n, n:]], 0),
                jnp.concatenate([halfway[n:, :n], halfway[n:, n:]], 0),
            ],
            1,
        )
        result = matmul(left, stacked).astype(jnp.bfloat16).astype(jnp.float32)
        out += [(result[:n, :n], result[n:, :n]), (result[:n, n:], result[n:, n:])]
    return out


def main_kernel(
    row_ref, col_ref, live_ref,
    tile_ref, rim_ref, probe_ref, cos_ref, sin_ref, fwd_ref, bwd_ref, measured_ref,
    object_ref, rim_out_ref, probe_out_ref,
    ext, acc, slab, win, waves, sems,
):
    planes, tile_rows, width = tile_ref.shape
    n = probe_ref.shape[-1]
    blocks = width // LANES
    slices = planes // 2
    capacity = measured_ref.shape[0]
    live = live_ref[0]

    loads = []
    for b in range(blocks):
        cols = pl.ds(b * LANES, LANES)
        loads.append(
            pltpu.make_async_copy(
                tile_ref.at[:, :, cols], ext.at[:, b, pl.ds(0, tile_rows), :], sems.at[2 * b]
            )
        )
        loads.append(
            pltpu.make_async_copy(
                rim_ref.at[:, :, cols], ext.at[:, b, pl.ds(tile_rows, n), :], sems.at[2 * b + 1]
            )
        )
    for load in loads:
        load.start()

    probe_out_ref[...] = jnp.zeros_like(probe_out_ref)

    @pl.loop(0, planes)
    def _(p):
        @pl.loop(0, blocks)
        def _(b):
            acc[p, b] = jnp.zeros(acc.shape[2:], jnp.float32)

    for load in loads:
        load.wait()

    lane = lax.broadcasted_iota(jnp.int32, (n, LANES), 1)
    lane_slab = lax.broadcasted_iota(jnp.int32, (n + 16, LANES), 1)

    def place(slot):
        row = row_ref[slot]
        col = col_ref[slot]
        block = jnp.minimum(col // LANES, blocks - 2)
        return row, block, col - block * LANES

    def cut(k, slot):
        row, block, shift = place(slot)
        base = pl.multiple_of(row // 16 * 16, 16)
        back = lax.rem(LANES - shift, LANES)

        @pl.loop(0, planes)
        def _(p):
            left = ext[p, block, pl.ds(base, n + 16), :].astype(jnp.float32)
            right = ext[p, block + 1, pl.ds(base, n + 16), :].astype(jnp.float32)
            left = pltpu.roll(left, back, 1)
            right = pltpu.roll(right, back, 1)
            slab[...] = jnp.where(lane_slab < LANES - shift, left, right)
            win[k, p] = slab[pl.ds(row - base, n), :]

    def deposit(k, slot):
        row, block, shift = place(slot)
        ahead = lax.rem(shift, LANES)

        @pl.loop(0, planes)
        def _(p):
            grad = pltpu.roll(win[k, p], ahead, 1)
            rows = pl.ds(row, n)
            acc[p, block, rows, :] += jnp.where(lane >= shift, grad, 0.0)
            acc[p, block + 1, rows, :] += jnp.where(lane < shift, grad, 0.0)

    @pl.loop(0, (live + GROUP - 1) // GROUP)
    def _(g):
        slots = [jnp.minimum(g * GROUP + k, capacity - 1) for k in range(GROUP)]
        for k in range(GROUP):
            cut(k, slots[k])
        ahead, behind = fwd_ref[...], bwd_ref[...]
        fields = [(probe_ref[0], probe_ref[1])] * GROUP
        for s in range(slices):
            for k in range(GROUP):
                w_re, w_im = fields[k]
                if s:
                    waves[k, s - 1, 0] = w_re
                    waves[k, s - 1, 1] = w_im
                o_re, o_im = win[k, 2 * s], win[k, 2 * s + 1]
                fields[k] = (w_re * o_re - w_im * o_im, w_re * o_im + w_im * o_re)
            fields = transform_pairs(fields, ahead, behind)
            if s + 1 < slices:
                h_re, h_im = cos_ref[...], sin_ref[...]
                fields = [(a * h_re - b * h_im, a * h_im + b * h_re) for a, b in fields]
                fields = transform_pairs(fields, behind, ahead)
        for k in range(GROUP):
            f_re, f_im = fields[k]
            weight = jnp.where(g * GROUP + k < live, 2.0, 0.0)
            target = measured_ref[slots[k]].astype(jnp.float32)
            inverse = lax.rsqrt(f_re * f_re + f_im * f_im + RIDGE)
            scale = weight * (1.0 - target * inverse)
            fields[k] = (scale * f_re, scale * f_im)
        for s in reversed(range(slices)):
            fields = transform_pairs_back(fields, behind, ahead)
            for k in range(GROUP):
                g_re, g_im = fields[k]
                if s:
                    w_re, w_im = waves[k, s - 1, 0], waves[k, s - 1, 1]
                else:
                    w_re, w_im = probe_ref[0], probe_ref[1]
                o_re, o_im = win[k, 2 * s], win[k, 2 * s + 1]
                fields[k] = (g_re * o_re + g_im * o_im, g_im * o_re - g_re * o_im)
                win[k, 2 * s] = g_re * w_re + g_im * w_im
                win[k, 2 * s + 1] = g_im * w_re - g_re * w_im
            if s:
                fields = transform_pairs_back(fields, ahead, behind)
                h_re, h_im = cos_ref[...], sin_ref[...]
                fields = [(a * h_re + b * h_im, b * h_re - a * h_im) for a, b in fields]
        for part in range(2):
            total = fields[0][part]
            for k in range(1, GROUP):
                total = total + fields[k][part]
            probe_out_ref[part] += total
        for k in range(GROUP):
            @pl.when(g * GROUP + k < live)
            def _():
                deposit(k, slots[k])

    stores = []
    for b in range(blocks):
        stores.append(
            pltpu.make_async_copy(
                acc.at[:, b, pl.ds(0, tile_rows), :],
                object_ref.at[:, :, pl.ds(b * LANES, LANES)],
                sems.at[b],
            )
        )
        stores[-1].start()

    @pl.loop(0, planes)
    def _(p):
        @pl.loop(0, blocks)
        def _(b):
            rim_out_ref[p, b] = acc[p, b, pl.ds(tile_rows, n), :].astype(jnp.bfloat16)

    for store in stores:
        store.wait()


def run_main(row, col, live, tile, rim, probe, h_re, h_im, ahead, behind, measured):
    planes, tile_rows, width = tile.shape
    n = probe.shape[-1]
    blocks = width // LANES
    any_spec = pl.BlockSpec(memory_space=pl.ANY)
    vmem = pl.BlockSpec(memory_space=pltpu.VMEM)
    smem = pl.BlockSpec(memory_space=pltpu.SMEM)
    return pl.pallas_call(
        main_kernel,
        out_shape=(
            jax.ShapeDtypeStruct((planes, tile_rows, width), jnp.float32),
            jax.ShapeDtypeStruct((planes, blocks, n, LANES), jnp.bfloat16),
            jax.ShapeDtypeStruct(probe.shape, jnp.float32),
        ),
        in_specs=[smem] * 3 + [any_spec] * 2 + [vmem] * 6,
        out_specs=(any_spec, vmem, vmem),
        scratch_shapes=[
            pltpu.VMEM((planes, blocks, tile_rows + n, LANES), jnp.bfloat16),
            pltpu.VMEM((planes, blocks, tile_rows + n, LANES), jnp.float32),
            pltpu.VMEM((n + 16, LANES), jnp.float32),
            pltpu.VMEM((GROUP, planes, n, n), jnp.float32),
            pltpu.VMEM((GROUP, planes // 2 - 1, 2, n, n), jnp.float32),
            pltpu.SemaphoreType.DMA((2 * blocks,)),
        ],
        compiler_params=pltpu.CompilerParams(vmem_limit_bytes=48 * 2**20),
    )(row, col, live, tile, rim, probe, h_re, h_im, ahead, behind, measured)


def add_kernel(grad_ref, rim_ref, out_ref):
    for b in range(rim_ref.shape[1]):
        cols = pl.ds(b * LANES, LANES)
        out_ref[0, :, cols] = grad_ref[0, :, cols] + rim_ref[0, b].astype(jnp.float32)


def add_rim(grad, rim):
    planes, _, width = grad.shape
    _, blocks, n, lanes = rim.shape
    block = pl.BlockSpec((1, n, width), lambda p: (p, 0, 0))
    return pl.pallas_call(
        add_kernel,
        grid=(planes,),
        out_shape=jax.ShapeDtypeStruct(grad.shape, grad.dtype),
        in_specs=[block, pl.BlockSpec((1, blocks, n, lanes), lambda p: (p, 0, 0, 0))],
        out_specs=block,
        input_output_aliases={0: 0},
        compiler_params=pltpu.CompilerParams(vmem_limit_bytes=16 * 2**20),
    )(grad, rim)


def local(transmission, probe_wavefield, phase_shift, offsets, live_counts, measured):
    slices, parts, tile_rows, width = transmission.shape
    n = probe_wavefield.shape[-1]
    capacity = offsets.shape[1]
    devices = lax.axis_size("ty")
    my_index = lax.axis_index("ty")
    tile = transmission.reshape(slices * parts, tile_rows, width)
    rim = passed_along(tile[:, :n, :], "ty", -1)
    ahead, behind = dft_tables(n)
    row = offsets[0] - my_index * tile_rows
    live = lax.dynamic_slice(live_counts, (my_index,), (1,))
    grad, rim_out, probe_part = run_main(
        row, offsets[1], live, tile, rim,
        probe_wavefield, jnp.cos(phase_shift), jnp.sin(phase_shift), ahead, behind, measured,
    )
    incoming = passed_along(rim_out, "ty", 1)
    probe_grad = summed_over(probe_part / math.sqrt(capacity * devices), "ty")
    grad = add_rim(grad, incoming)
    return (grad.reshape(slices, parts, tile_rows, width), probe_grad)


def solution(mesh):
    in_specs = (
        P(None, None, ("groups", "ty"), None),
        P("groups", None, None),
        P(),
        P(None, ("groups", "ty")),
        P("groups"),
        P(("groups", "ty"), None, None),
    )
    out_specs = (P(None, None, ("groups", "ty"), None), P("groups", None, None))
    return jax.shard_map(local, mesh=mesh, in_specs=in_specs, out_specs=out_specs, check_vma=False)
```

time: 347 us -> 108 us (0.31)
  local copies, waits for them, and re-layouts: 140 us -> 4.01 us
  waiting for transfers between devices: 103 us -> 57.3 us
  other arithmetic: 37.2 us -> 0.76 us
  Pallas kernels: 0 us -> 35.4 us
  loops' own time: 31.3 us -> 0 us
  between operations: 14.7 us -> 0.77 us
  matrix products: 9.75 us -> 0 us
    psum x1 -> x0, waiting for transfers between devices: 82 us -> none  [local(): probe_grad = lax.psum(probe_part, 'ty') / math.sqrt(capacity * devices)]
    dynamic_update_slice x8 -> x0, local copies, waits for them, and re-layouts: 59.9 us -> none  [deposit(): lax.dynamic_update_slice(grad_acc, current + slot_grads[slot_id], corner)]
    pallas_call x0 -> x2, Pallas kernels: none -> 35.4 us  [the longest x1 28.7 us: run_main(): pl.pallas_call(main_kernel, out_shape=(jax.ShapeDtypeStruct((planes, tile...]
    ppermute x0 -> x4, waiting for transfers between devices: none -> 34.3 us  [summed_over(): other = lax.ppermute(block, axis, route)]
    gather x40 -> x0, local copies, waits for them, and re-layouts: 33.5 us -> none
    another operation x2 -> x0, loops' own time: 31.3 us -> none  [the longest x1 31.2 us: local(): lax.fori_loop(0, capacity, deposit, jnp.zeros((slices, 2, tile_rows + pat...]
    dynamic_slice x33 -> x1, local copies, waits for them, and re-layouts: 20.2 us -> 0.59 us  [local(): live = lax.dynamic_slice(live_counts, (my_index,), (1,))]
    add x8 -> x1, other arithmetic: 11.9 us -> 0.67 us  [summed_over(): block = block.astype(jnp.float32) + other.astype(jnp.float32)]
  transfers between devices with their start and end apart: 3 -> 6, of which waited for: 2 -> 5; matrix products, arithmetic and copies ran while one was open for 4% -> 1% of each run, Pallas kernels for 0% -> 0%
where the time goes in v1:
time: 108 us; the launch traced here: 107 us
  waiting for transfers between devices  57.3 us (53%)
  Pallas kernels  35.4 us (33%)
  starting transfers between devices  8.31 us (8%)
  local copies, waits for them, and re-layouts  4.01 us (4%)
    ppermute x4, waiting for transfers between devices, summed_over(): other = lax.ppermute(block, axis, route)  34.3 us
    pallas_call x1, Pallas kernels, run_main(): pl.pallas_call(main_kernel, out_shape=(jax.ShapeDtypeStruct((planes, tile...  28.7 us
    ppermute x2, waiting for transfers between devices, passed_along(): return lax.ppermute(block, axis, route)  23 us
    pallas_call x1, Pallas kernels, add_rim(): pl.pallas_call(add_kernel, grid=(planes,), out_shape=jax.ShapeDtypeStruct...  6.67 us
    ppermute x2, starting transfers between devices, passed_along(): return lax.ppermute(block, axis, route)  4.66 us
    ppermute x4, starting transfers between devices, summed_over(): other = lax.ppermute(block, axis, route)  3.65 us
    slice x1, local copies, waits for them, and re-layouts, local(): rim = passed_along(tile[:, :n, :], 'ty', -1)  3.15 us
  transfers between devices with their start and end apart: 6, of which 5 were waited for; matrix products, arithmetic and copies ran while one was open for 1% of the time, Pallas kernels for 0%

profile of v1, /device:TPU:8, one launch (start us, length us, event | category | flops | bytes accessed | tf_op | source)
XLA Modules:
  0.0 106.6 jit_solution(16753195303653189677)
XLA Ops:
  0.6 0.0 copy-start.6
  0.6 0.0 copy-start.5
  0.7 0.0 copy-start.4
  0.7 0.0 copy-start.2
  0.7 0.0 copy-start.3
  0.7 3.1 %slice.12 = bf16[8,128,1024]{2,1,0:T(8,128)(2,1)} slice(bf16[8,256,1024]{2,1,0:T(8,128)(2,1)} %bitcast.6), slice={[0:8], [0:128], [0:1024]} | slice | bytes 4194304 | tf_op jit(solution)/shard_map/slice | solution.py:307
  3.9 2.7 %collective-permute-start = (bf16[8,128,1024]{2,1,0:T(8,128)(2,1)}, bf16[8,128,1024]{2,1,0:T(8,128)(2,1)S(1)}, u32[]{:S(2)}, u32[]{:S(2)}) collective-permute-start(bf16[8,128,1024]{2,1,0:T(8,128)(2,1)} %slice.12), channel_id=1, source_target_pairs={{1,0},{2,1},{3,2},{4,3},{5,4},{6,5},{7,6},{8,7},{9,8},{10,9},{11,1... | collective-permute-start | bytes 6291464 | tf_op jit(solution)/shard_map/ppermute | solution.py:19
  6.6 0.6 dynamic_slice.3.live_ref
  7.2 0.2 fusion
  7.5 23.0 %collective-permute-done.rim_ref = bf16[8,128,1024]{2,1,0:T(8,128)(2,1)S(1)} collective-permute-done((bf16[8,128,1024]{2,1,0:T(8,128)(2,1)}, bf16[8,128,1024]{2,1,0:T(8,128)(2,1)S(1)}, u32[]{:S(2)}, u32[]{:S(2)}) %collective-permute-start) | collective-permute-done | bytes 2097184 | tf_op jit(solution)/shard_map/ppermute | solution.py:19
  30.5 0.0 copy-done.2
  30.5 28.7 %shard_map.95 = (f32[8,256,1024]{2,1,0:T(8,128)}, bf16[8,8,128,128]{3,2,1,0:T(8,128)(2,1)S(1)}, f32[2,128,128]{2,1,0:T(8,128)S(1)}) custom-call(s32[8]{0:T(128)S(1)} %get-tuple-element.11.row_ref, s32[8]{0:T(128)S(1)} %get-tuple-element.10.col_ref, s32[1]{0:T(128)} %dynamic_slice.3.live_ref, bf16[8,256,1024]{2,1,0:T(8,128)(2,1)} %bitcast.7, ...), custom_call_target="tpu_custom_call" | custom-call | tf_op jit(solution)/shard_map/pallas_call | solution.py:258
  59.2 1.9 %collective-permute-start.1 = (bf16[8,8,128,128]{3,2,1,0:T(8,128)(2,1)S(1)}, bf16[8,8,128,128]{3,2,1,0:T(8,128)(2,1)S(1)}, u32[]{:S(2)}, u32[]{:S(2)}) collective-permute-start(bf16[8,8,128,128]{3,2,1,0:T(8,128)(2,1)S(1)} %get-tuple-element.6), channel_id=1, source_target_pairs={{0,1},{1,2},{2,3},{3,4},{4,5},{5,6},{6,7},{7,8},{8,9},{9,10},{10,1... | collective-permute-start | bytes 6291464 | tf_op jit(solution)/shard_map/ppermute | solution.py:19
  61.2 1.6 %collective-permute-start.2 = (bf16[2,128,128]{2,1,0:T(8,128)(2,1)S(1)}, bf16[2,128,128]{2,1,0:T(8,128)(2,1)S(1)}, u32[]{:S(2)}, u32[]{:S(2)}) collective-permute-start(bf16[2,128,128]{2,1,0:T(8,128)(2,1)S(1)} %multiply_convert_fusion), channel_id=1, source_target_pairs={{0,1},{1,0},{2,3},{3,2},{4,5},{5,4},{6,7},{7,6},{8,9},{9,8},{10,11... | collective-permute-start | bytes 196616 | tf_op jit(solution)/shard_map/ppermute | solution.py:30
  62.7 2.3 %collective-permute-done.2 = bf16[2,128,128]{2,1,0:T(8,128)(2,1)S(1)} collective-permute-done((bf16[2,128,128]{2,1,0:T(8,128)(2,1)S(1)}, bf16[2,128,128]{2,1,0:T(8,128)(2,1)S(1)}, u32[]{:S(2)}, u32[]{:S(2)}) %collective-permute-start.2) | collective-permute-done | bytes 65568 | tf_op jit(solution)/shard_map/ppermute | solution.py:30
  65.0 1.5 %collective-permute-start.3 = (bf16[2,128,128]{2,1,0:T(8,128)(2,1)S(1)}, bf16[2,128,128]{2,1,0:T(8,128)(2,1)S(1)}, u32[]{:S(2)}, u32[]{:S(2)}) collective-permute-start(bf16[2,128,128]{2,1,0:T(8,128)(2,1)S(1)} %add_convert_fusion.2), channel_id=1, source_target_pairs={{0,2},{1,3},{2,0},{3,1},{4,6},{5,7},{6,4},{7,5},{8,10},{9,11},{10,... | collective-permute-start | bytes 196616 | tf_op jit(solution)/shard_map/ppermute | solution.py:30
  66.5 23.1 %collective-permute-done.3 = bf16[2,128,128]{2,1,0:T(8,128)(2,1)S(1)} collective-permute-done((bf16[2,128,128]{2,1,0:T(8,128)(2,1)S(1)}, bf16[2,128,128]{2,1,0:T(8,128)(2,1)S(1)}, u32[]{:S(2)}, u32[]{:S(2)}) %collective-permute-start.3) | collective-permute-done | bytes 65568 | tf_op jit(solution)/shard_map/ppermute | solution.py:30
  89.7 0.1 collective-permute-start.4
  89.7 4.3 %collective-permute-done.4 = bf16[2,128,128]{2,1,0:T(8,128)(2,1)S(1)} collective-permute-done((bf16[2,128,128]{2,1,0:T(8,128)(2,1)S(1)}, bf16[2,128,128]{2,1,0:T(8,128)(2,1)S(1)}, u32[]{:S(2)}, u32[]{:S(2)}) %collective-permute-start.4) | collective-permute-done | bytes 65568 | tf_op jit(solution)/shard_map/ppermute | solution.py:30
  94.0 0.6 collective-permute-start.5
  94.6 4.7 %collective-permute-done.5 = bf16[2,128,128]{2,1,0:T(8,128)(2,1)S(1)} collective-permute-done((bf16[2,128,128]{2,1,0:T(8,128)(2,1)S(1)}, bf16[2,128,128]{2,1,0:T(8,128)(2,1)S(1)}, u32[]{:S(2)}, u32[]{:S(2)}) %collective-permute-start.5) | collective-permute-done | bytes 65568 | tf_op jit(solution)/shard_map/ppermute | solution.py:30
  99.2 0.7 convert_add_fusion
  99.9 0.0 collective-permute-done.1.rim_ref
  99.9 6.7 %shard_map.96 = f32[8,256,1024]{2,1,0:T(8,128)} custom-call(f32[8,256,1024]{2,1,0:T(8,128)} %get-tuple-element.5.grad_ref, bf16[8,8,128,128]{3,2,1,0:T(8,128)(2,1)S(1)} %collective-permute-done.1.rim_ref), custom_call_target="tpu_custom_call", output_to_operand_aliasing={{}: (0, {})} | custom-call | tf_op jit(solution)/shard_map/pallas_call | solution.py:289
  (13 shorter events, 0.1 us)
Async XLA Ops:
  0.6 6.0 %copy-start.6 = (s32[16]{0:T(128)S(1)}, s32[16]{0:T(128)}, u32[]{:S(2)}) copy-start(s32[16]{0:T(128)} %param.12) | copy-start | bytes 196
  0.6 6.6 %copy-start.5 = (s32[2,8]{1,0:T(2,128)S(1)}, s32[2,8]{1,0:T(2,128)}, u32[]{:S(2)}) copy-start(s32[2,8]{1,0:T(2,128)} %param.11) | copy-start | bytes 196
  0.7 6.6 %copy-start.4 = (f32[128,128]{1,0:T(8,128)S(1)}, f32[128,128]{1,0:T(8,128)}, u32[]{:S(2)}) copy-start(f32[128,128]{1,0:T(8,128)} %param.10) | copy-start | bytes 196612
  0.7 29.8 %copy-start = (bf16[8,128,128]{2,1,0:T(8,128)(2,1)S(1)}, bf16[8,128,128]{2,1,0:T(8,128)(2,1)}, u32[]{:S(2)}) copy-start(bf16[8,128,128]{2,1,0:T(8,128)(2,1)} %measured_ref.1) | copy-start | bytes 786436
  0.7 29.8 %copy-start.1 = (f32[2,128,128]{2,1,0:T(8,128)S(1)}, f32[2,128,128]{2,1,0:T(8,128)}, u32[]{:S(2)}) copy-start(f32[2,128,128]{2,1,0:T(8,128)} %probe_ref.1) | copy-start | bytes 393220
  0.7 29.8 %copy-start.2 = (bf16[256,256]{1,0:T(8,128)(2,1)S(1)}, bf16[256,256]{1,0:T(8,128)(2,1)}, u32[]{:S(2)}) copy-start(bf16[256,256]{1,0:T(8,128)(2,1)} %constant.18.clone.bwd_ref) | copy-start | bytes 393220
  0.7 29.8 %copy-start.3 = (bf16[256,256]{1,0:T(8,128)(2,1)S(1)}, bf16[256,256]{1,0:T(8,128)(2,1)}, u32[]{:S(2)}) copy-start(bf16[256,256]{1,0:T(8,128)(2,1)} %constant.17.clone.fwd_ref) | copy-start | bytes 393220
  3.9 26.6 %collective-permute-start = (bf16[8,128,1024]{2,1,0:T(8,128)(2,1)}, bf16[8,128,1024]{2,1,0:T(8,128)(2,1)S(1)}, u32[]{:S(2)}, u32[]{:S(2)}) collective-permute-start(bf16[8,128,1024]{2,1,0:T(8,128)(2,1)} %slice.12), channel_id=1, source_target_pairs={{1,0},{2,1},{3,2},{4,3},{5,4},{6,5},{7,6},{8,7},{9,8},{10,9},{11,1... | collective-permute-start | bytes 6291464 | tf_op jit(solution)/shard_map/ppermute | solution.py:19
  59.2 40.7 %collective-permute-start.1 = (bf16[8,8,128,128]{3,2,1,0:T(8,128)(2,1)S(1)}, bf16[8,8,128,128]{3,2,1,0:T(8,128)(2,1)S(1)}, u32[]{:S(2)}, u32[]{:S(2)}) collective-permute-start(bf16[8,8,128,128]{3,2,1,0:T(8,128)(2,1)S(1)} %get-tuple-element.6), channel_id=1, source_target_pairs={{0,1},{1,2},{2,3},{3,4},{4,5},{5,6},{6,7},{7,8},{8,9},{9,10},{10,1... | collective-permute-start | bytes 6291464 | tf_op jit(solution)/shard_map/ppermute | solution.py:19
  61.2 3.8 %collective-permute-start.2 = (bf16[2,128,128]{2,1,0:T(8,128)(2,1)S(1)}, bf16[2,128,128]{2,1,0:T(8,128)(2,1)S(1)}, u32[]{:S(2)}, u32[]{:S(2)}) collective-permute-start(bf16[2,128,128]{2,1,0:T(8,128)(2,1)S(1)} %multiply_convert_fusion), channel_id=1, source_target_pairs={{0,1},{1,0},{2,3},{3,2},{4,5},{5,4},{6,7},{7,6},{8,9},{9,8},{10,11... | collective-permute-start | bytes 196616 | tf_op jit(solution)/shard_map/ppermute | solution.py:30
  65.0 24.6 %collective-permute-start.3 = (bf16[2,128,128]{2,1,0:T(8,128)(2,1)S(1)}, bf16[2,128,128]{2,1,0:T(8,128)(2,1)S(1)}, u32[]{:S(2)}, u32[]{:S(2)}) collective-permute-start(bf16[2,128,128]{2,1,0:T(8,128)(2,1)S(1)} %add_convert_fusion.2), channel_id=1, source_target_pairs={{0,2},{1,3},{2,0},{3,1},{4,6},{5,7},{6,4},{7,5},{8,10},{9,11},{10,... | collective-permute-start | bytes 196616 | tf_op jit(solution)/shard_map/ppermute | solution.py:30
  89.7 4.3 %collective-permute-start.4 = (bf16[2,128,128]{2,1,0:T(8,128)(2,1)S(1)}, bf16[2,128,128]{2,1,0:T(8,128)(2,1)S(1)}, u32[]{:S(2)}, u32[]{:S(2)}) collective-permute-start(bf16[2,128,128]{2,1,0:T(8,128)(2,1)S(1)} %add_convert_fusion.1), channel_id=1, source_target_pairs={{0,4},{1,5},{2,6},{3,7},{4,0},{5,1},{6,2},{7,3},{8,12},{9,13},{10,... | collective-permute-start | bytes 196616 | tf_op jit(solution)/shard_map/ppermute | solution.py:30
  94.0 5.2 %collective-permute-start.5 = (bf16[2,128,128]{2,1,0:T(8,128)(2,1)S(1)}, bf16[2,128,128]{2,1,0:T(8,128)(2,1)S(1)}, u32[]{:S(2)}, u32[]{:S(2)}) collective-permute-start(bf16[2,128,128]{2,1,0:T(8,128)(2,1)S(1)} %add_convert_fusion), channel_id=1, source_target_pairs={{0,8},{1,9},{2,10},{3,11},{4,12},{5,13},{6,14},{7,15},{8,0},{9,1},... | collective-permute-start | bytes 196616 | tf_op jit(solution)/shard_map/ppermute | solution.py:30
